TPU v7x, 32 devices: a whole 2x2x4 slice. The times are simulated.
32 devices in a mesh: seg: 4 (over y, x), sec: 8 (over z, core).
Axes of the slice: x: 2, y: 2, z: 4, core: 2. Of those that a mesh axis runs over, the one named last changes fastest.
Arguments:
- psi: bfloat16 [4, 8, 16, 128, 128], P('seg', 'sec'), may hold values from -6 to 6
- env_build: bfloat16 [4, 8, 12, 128, 128], P('seg', 'sec'), may hold values from -0.5 to 0.5
- env_right: bfloat16 [4, 8, 12, 128, 128], P('seg', 'sec'), may hold values from -0.5 to 0.5
- site_left: bfloat16 [12, 12, 4, 4], replicated, may hold values from -0.4375 to 0.4375
- site_right: bfloat16 [12, 12, 4, 4], replicated, may hold values from -0.4375 to 0.4375
- charge: int32 [16], replicated, may hold values from 0 to 7
- rank: int32 [8], P('sec'), may hold values from 64 to 128
Outputs:
- state: bfloat16 [4, 8, 16, 128, 128], P('seg', 'sec')
- energy: float32 [4], P('seg')
- sector_weight: float32 [4, 8], P('seg', 'sec')
All inputs are finite; a program needn't handle non-finite values.
Results may differ from a plain program's by a relative error of at most 0.012.
Values may be sent and summed in bfloat16 or wider, within the bound.
A program may use at most 128 MiB of HBM per device.

v0:
```python
import jax
import jax.numpy as jnp
from jax import lax
from jax.sharding import PartitionSpec as P

ITERS = 2


def from_behind(value, axis, steps):
    count = lax.axis_size(axis)
    initial, last = (max(0, -steps), min(count, count - steps))
    return lax.ppermute(value, axis, [(source, source + steps) for source in range(initial, last)])


def entering(value, axis, join, neutral):
    count, mine = (lax.axis_size(axis), lax.axis_index(axis))
    pieces = lax.all_gather(value, axis)
    total = jnp.full_like(value, 0) + jnp.asarray(neutral, value.dtype)

    def lap(position, total):
        longer = join(total, pieces[position])
        return jnp.where(position < mine, longer, total)

    return lax.fori_loop(0, count - 1, lap, total)


def pair_mpo(site_left, site_right):
    joined = jnp.einsum(
        "lmxs,mwyt->lwxyst", site_left, site_right, preferred_element_type=jnp.float32
    )
    width = joined.shape[0]
    local = joined.shape[2]
    return joined.reshape(width, width, local * local, local * local).astype(jnp.bfloat16)


def apply_local(x_sector, lenv, renv, mpo, left_row):
    rows = x_sector.shape[1]
    blocks = 4
    step_rows = rows // blocks
    total = jnp.zeros(x_sector.shape, jnp.float32)
    for block in range(blocks):
        lo_row = block * step_rows
        piece = x_sector[:, lo_row : lo_row + step_rows, :]
        first = jnp.einsum("pab,wbc->pwac", piece, renv, preferred_element_type=jnp.float32).astype(
            jnp.bfloat16
        )
        third = jnp.einsum(
            "lwqp,pwac->lqac", mpo, first, preferred_element_type=jnp.float32
        ).astype(jnp.bfloat16)
        chosen = jnp.take(lenv[:, :, :, lo_row : lo_row + step_rows], left_row, axis=0)
        total = total + jnp.einsum(
            "qlxa,lqac->qxc", chosen, third, preferred_element_type=jnp.float32
        )
    return total


def shards(psi, env_build, env_right, site_left, site_right, charge, rank):
    nsec = lax.axis_size("sec")
    sector = lax.axis_index("sec")
    segment = lax.axis_index("seg")
    mpo = pair_mpo(site_left, site_right)
    left_row = (sector - charge) % nsec
    own = env_build[0]
    whole = lax.all_gather(own, "sec", axis=0, tiled=True)
    moved = from_behind(whole, "seg", 1)
    lenv = jnp.where(segment == 0, whole, moved)
    renv = env_right[0, 0]
    x = psi[0, 0]
    width = x.shape[2]
    keep = (jnp.arange(width) < rank[0])[None, None, :]
    count = float(nsec * x.shape[0] * x.shape[1] * width)
    energy = jnp.zeros((), jnp.float32)
    squares = jnp.ones((), jnp.float32)
    total = jnp.ones((), jnp.float32)
    for step in range(ITERS):
        h = apply_local(x, lenv, renv, mpo, left_row)
        xf = x.astype(jnp.float32)
        u = jnp.where(keep, xf - 0.5 * h, 0.0)
        squares = jnp.sum(u * u)
        total, inner, self_sum = lax.psum((squares, jnp.sum(xf * h), jnp.sum(xf * xf)), "sec")
        energy = inner / self_sum
        x = (u * lax.rsqrt(total / count + 1e-06)).astype(jnp.bfloat16)
    share = jnp.log(float(nsec) * squares / total)
    before = entering(share, "seg", lambda early, late: early + late, jnp.zeros((), jnp.float32))
    summed = before + share
    return (x[None, None], energy.reshape(1), summed.reshape(1, 1))


def solution(mesh):
    return jax.shard_map(
        shards,
        mesh=mesh,
        in_specs=(
            P("seg", "sec", None, None, None),
            P("seg", "sec", None, None, None),
            P("seg", "sec", None, None, None),
            P(),
            P(),
            P(),
            P("sec"),
        ),
        out_specs=(P("seg", "sec", None, None, None), P("seg"), P("seg", "sec")),
        check_vma=False,
    )
```

profile of v0, /device:TPU:4, one launch (start us, length us, event | category | flops | bytes accessed | tf_op | source)
XLA Modules:
  0.0 238.7 jit_solution(13150958383151653073)
XLA Ops:
  8.0 1.3 fusion.36
  9.3 2.3 copy.33
  11.5 1.3 copy.69
  14.8 34.4 %all-gather.3.cloned.1.call-done = bf16[8,1,12,128,128]{4,3,2,1,0:T(8,128)(2,1)} async-done(((bf16[1,1,12,128,128]{4,3,2,1,0:T(8,128)(2,1)}), bf16[8,1,12,128,128]{4,3,2,1,0:T(8,128)(2,1)}) %all-gather.3.cloned.1.call-update) | async-done | bytes 3145744 | tf_op jit(solution)/shard_map/all_gather | solution.py:64
  49.2 3.4 %collective-permute-start = (bf16[8,12,128,128]{3,2,1,0:T(8,128)(2,1)}, bf16[8,12,128,128]{3,2,1,0:T(8,128)(2,1)S(1)}, u32[]{:S(2)}, u32[]{:S(2)}) collective-permute-start(bf16[8,12,128,128]{3,2,1,0:T(8,128)(2,1)} %bitcast.205), channel_id=1, source_target_pairs={{0,8},{8,16},{16,24},{1,9},{9,17},{17,25},{2,10},{10,18},{18,26},{... | collective-permute-start | bytes 9437192 | tf_op jit(solution)/shard_map/ppermute | solution.py:12
  54.3 2.2 bitcast_convert_fusion.5
  56.5 2.3 bitcast_convert_fusion.6
  58.9 2.3 bitcast_convert_fusion.4
  61.1 2.2 bitcast_convert_fusion.7
  63.3 59.1 %collective-permute-done = bf16[8,12,128,128]{3,2,1,0:T(8,128)(2,1)S(1)} collective-permute-done((bf16[8,12,128,128]{3,2,1,0:T(8,128)(2,1)}, bf16[8,12,128,128]{3,2,1,0:T(8,128)(2,1)S(1)}, u32[]{:S(2)}, u32[]{:S(2)}) %collective-permute-start) | collective-permute-done | bytes 3145760 | tf_op jit(solution)/shard_map/ppermute | solution.py:12
  122.8 5.6 %fusion.111 = (bf16[8,12,128,32]{3,2,1,0:T(8,128)(2,1)S(1)}, bf16[8,12,128,32]{3,2,1,0:T(8,128)(2,1)}, bf16[8,12,128,32]{3,2,1,0:T(8,128)(2,1)}, bf16[8,12,128,32]{3,2,1,0:T(8,128)(2,1)}) fusion(bf16[8,12,128,128]{3,2,1,0:T(8,128)(2,1)S(1)} %broadcast_select_fusion.4), kind=kLoop, calls=%fused_computation.125 | loop fusion | bytes 6291456 | tf_op jit(solution)/shard_map/slice | solution.py:50
  128.4 5.9 %gather_fusion.2 = bf16[16,12,128,32]{3,2,1,0:T(8,128)(2,1)} fusion(bf16[8,12,128,32]{3,2,1,0:T(8,128)(2,1)} %get-tuple-element.102, s32[1024]{0:T(1024)S(1)} %pad_clamp_fusion), kind=kCustom, calls=%fused_computation.2.clone | custom fusion | bytes 3145792 | tf_op jit(solution)/shard_map/jit(_take)/gather | solution.py:50
  134.3 5.8 %gather_fusion.1 = bf16[16,12,128,32]{3,2,1,0:T(8,128)(2,1)} fusion(bf16[8,12,128,32]{3,2,1,0:T(8,128)(2,1)} %get-tuple-element.103, s32[1024]{0:T(1024)S(1)} %pad_clamp_fusion), kind=kCustom, calls=%fused_computation.1.clone | custom fusion | bytes 3145792 | tf_op jit(solution)/shard_map/jit(_take)/gather | solution.py:50
  140.1 5.9 %gather_fusion.3 = bf16[16,12,128,32]{3,2,1,0:T(8,128)(2,1)} fusion(bf16[8,12,128,32]{3,2,1,0:T(8,128)(2,1)} %get-tuple-element.101, s32[1024]{0:T(1024)S(1)} %pad_clamp_fusion), kind=kCustom, calls=%fused_computation.3.clone | custom fusion | bytes 3145792 | tf_op jit(solution)/shard_map/jit(_take)/gather | solution.py:50
  146.0 4.0 %gather_fusion = bf16[16,12,128,32]{3,2,1,0:T(8,128)(2,1)} fusion(bf16[8,12,128,32]{3,2,1,0:T(8,128)(2,1)S(1)} %get-tuple-element.100, s32[1024]{0:T(1024)S(1)} %pad_clamp_fusion), kind=kCustom, calls=%fused_computation.clone | custom fusion | bytes 3145792 | tf_op jit(solution)/shard_map/jit(_take)/gather | solution.py:50
  150.0 5.2 %fusion.43 = f32[16,128,128]{2,1,0:T(8,128)S(1)} fusion(bf16[12,16,32,128]{3,1,2,0:T(8,128)(2,1)} %bitcast_convert_fusion.5, bf16[16,12,128,32]{3,2,1,0:T(8,128)(2,1)} %gather_fusion.2, pred[16]{0:T(512)(128)(4,1)S(1)} %get-tuple-element.98), kind=kOutput, calls=%fused_computation.68 | convolution fusion | flops 202113024 | bytes 4194320 | tf_op jit(solution)/shard_map/qlxa,lqac->qxc/dot_general | solution.py:51
  155.2 4.8 %fusion.49 = f32[16,128,128]{2,1,0:T(8,128)S(1)} fusion(bf16[12,16,32,128]{3,1,2,0:T(8,128)(2,1)S(1)} %copy-done.9, bf16[16,12,128,32]{3,2,1,0:T(8,128)(2,1)} %gather_fusion.1, pred[16]{0:T(512)(128)(4,1)S(1)} %get-tuple-element.98), kind=kOutput, calls=%fused_computation.70 | convolution fusion | flops 202113024 | bytes 4194320 | tf_op jit(solution)/shard_map/qlxa,lqac->qxc/dot_general | solution.py:51
  160.0 1.8 fusion.37
  162.2 3.0 %multiply_reduce_fusion.1 = (f32[]{:T(128)}, f32[16,128,128]{2,1,0:T(8,128)S(1)}) fusion(f32[16,128,128]{2,1,0:T(8,128)S(1)} %fusion.37, f32[16,128,128]{2,1,0:T(8,128)S(1)} %fusion.43, f32[16,128,128]{2,1,0:T(8,128)S(1)} %fusion.49, bf16[12,16,32,128]{3,1,2,0:T(8,128)(2,1)S(1)} %copy-done.8, bf16[16,12,128,32]{3,2,1,0:T(8,128)(2,1)S(1)} %bitcast.193, ...), kind=kOutput, calls=%fused_computation.89 | convolution fusion | flops 204472320 | bytes 7864468 | tf_op jit(solution)/shard_map/qlxa,lqac->qxc/dot_general | solution.py:51
  165.2 14.5 %psum.28 = f32[]{:T(128)} all-reduce(f32[]{:T(128)} %get-tuple-element.104), channel_id=1, replica_groups=mesh['seg'=4,'sec'=8] {'sec'}, use_global_device_ids=true, to_apply=%region_1.3 | all-reduce | flops 1 | bytes 8 | tf_op jit(solution)/shard_map/psum | solution.py:80
  182.8 1.4 bitcast_convert_fusion.2
  185.2 1.8 fusion.52
  187.0 1.4 bitcast_convert_fusion.1
  188.4 1.8 fusion.46
  190.3 1.4 bitcast_convert_fusion.3
  191.7 1.4 bitcast_convert_fusion
  193.5 2.1 fusion.40
  195.6 3.2 %fusion.89 = (f32[]{:T(128)}, f32[]{:T(128)}, f32[]{:T(128)}, f32[16,128,128]{2,1,0:T(8,128)S(1)}) fusion(bf16[16,128,128]{2,1,0:T(8,128)(2,1)S(1)} %multiply_convert_fusion.1, pred[128]{0:T(512)(128)(4,1)S(1)} %iota_compare_fusion, f32[16,128,128]{2,1,0:T(8,128)S(1)} %fusion.40, f32[16,128,128]{2,1,0:T(8,128)S(1)} %fusion.46, ...), kind=kOutput, calls=%fused_computation.84 | convolution fusion | flops 205520896 | bytes 7864476 | tf_op jit(solution)/shard_map/qlxa,lqac->qxc/dot_general | solution.py:51
  199.4 14.3 %all-reduce.1 = (f32[]{:T(128)}, f32[]{:T(128)}, f32[]{:T(128)}) all-reduce(f32[]{:T(128)} %get-tuple-element.85, f32[]{:T(128)} %get-tuple-element.84, f32[]{:T(128)} %get-tuple-element.86), channel_id=1, replica_groups=mesh['seg'=4,'sec'=8] {'sec'}, use_global_device_ids=true, to_apply=%region_3.5 | all-reduce | flops 3 | bytes 24 | tf_op jit(solution)/shard_map/psum | solution.py:80
  215.6 8.0 %all-reduce = f32[4]{0:T(128)S(1)} all-reduce(f32[4]{0:T(128)S(1)} %dynamic-update-slice), channel_id=1, replica_groups=mesh['seg'=4,'sec'=8] {'seg'}, use_global_device_ids=true, to_apply=%add | all-reduce | flops 4 | bytes 32
  223.7 3.5 %while.13 = (s32[]{:T(128)}, f32[]{:T(128)}, s32[]{:T(128)}, f32[4]{0:T(128)S(1)}, s32[]{:T(128)}) while((s32[]{:T(128)}, f32[]{:T(128)}, s32[]{:T(128)}, f32[4]{0:T(128)S(1)}, s32[]{:T(128)}) %tuple.41), condition=%wide.region_9.11_spmd, body=%wide.region_8.10_spmd.sunk | while | flops 5 | bytes 107 | solution.py:24
  228.6 1.0 fusion.91
  (73 shorter events, 10.6 us)
Async XLA Ops:
  7.2 7.1 %copy-start = (bf16[1,1,12,128,128]{4,3,2,1,0:T(8,128)(2,1)S(1)}, bf16[1,1,12,128,128]{4,3,2,1,0:T(8,128)(2,1)}, u32[]{:S(2)}) copy-start(bf16[1,1,12,128,128]{4,3,2,1,0:T(8,128)(2,1)} %param.13) | copy-start | bytes 1179652
  7.2 6.4 %copy-start.7 = (u32[32]{0:T(128)S(1)}, u32[32]{0:T(128)}, u32[]{:S(2)}) copy-start(u32[32]{0:T(128)} %constant.73) | copy-start | bytes 388
  7.2 7.0 %copy-start.6 = (s32[16]{0:T(128)S(1)}, s32[16]{0:T(128)}, u32[]{:S(2)}) copy-start(s32[16]{0:T(128)} %param.16) | copy-start | bytes 196
  7.2 7.0 %copy-start.4 = (bf16[1,1,16,128,128]{4,3,2,1,0:T(8,128)(2,1)S(1)}, bf16[1,1,16,128,128]{4,3,2,1,0:T(8,128)(2,1)}, u32[]{:S(2)}) copy-start(bf16[1,1,16,128,128]{4,3,2,1,0:T(8,128)(2,1)} %param.11) | copy-start | bytes 1572868
  7.2 42.0 %all-gather.3.cloned.1.call-start = ((), (), s32[]{:S(2)}) async-start(), calls=%async_computation | async-start | bytes 3538944 | tf_op jit(solution)/shard_map/all_gather | solution.py:64
  12.9 48.2 %copy-start.2 = (bf16[12,12,16,16,1]{3,2,1,4,0:T(8,128)(2,1)}, bf16[12,12,16,16,1]{3,2,1,4,0:T(8,128)(2,1)S(1)}, u32[]{:S(2)}) copy-start(bf16[12,12,16,16,1]{3,2,1,4,0:T(8,128)(2,1)S(1)} %copy.69) | copy-start | bytes 221188
  49.2 73.2 %collective-permute-start = (bf16[8,12,128,128]{3,2,1,0:T(8,128)(2,1)}, bf16[8,12,128,128]{3,2,1,0:T(8,128)(2,1)S(1)}, u32[]{:S(2)}, u32[]{:S(2)}) collective-permute-start(bf16[8,12,128,128]{3,2,1,0:T(8,128)(2,1)} %bitcast.205), channel_id=1, source_target_pairs={{0,8},{8,16},{16,24},{1,9},{9,17},{17,25},{2,10},{10,18},{18,26},{... | collective-permute-start | bytes 9437192 | tf_op jit(solution)/shard_map/ppermute | solution.py:12
  61.1 61.3 %copy-start.1 = (bf16[8,1,12,128,128]{4,3,2,1,0:T(8,128)(2,1)S(1)}, bf16[8,1,12,128,128]{4,3,2,1,0:T(8,128)(2,1)}, u32[]{:S(2)}) copy-start(bf16[8,1,12,128,128]{4,3,2,1,0:T(8,128)(2,1)} %all-gather.3.cloned.1.call-done) | copy-start | bytes 9437188
  150.0 5.2 %copy-start.9 = (bf16[12,16,32,128]{3,1,2,0:T(8,128)(2,1)S(1)}, bf16[12,16,32,128]{3,1,2,0:T(8,128)(2,1)}, u32[]{:S(2)}) copy-start(bf16[12,16,32,128]{3,1,2,0:T(8,128)(2,1)} %bitcast_convert_fusion.6) | copy-start | bytes 4718596
  150.0 10.0 %slice-start.4 = ((s8[6291456]{0:T(1024)(128)(4,1)}), s8[4194304]{0:T(1024)(128)(4,1)S(1)}, s32[]{:S(2)}) async-start(s8[6291456]{0:T(1024)(128)(4,1)} %bitcast.196), calls=%async_computation.5 | async-start | bytes 8388608
  155.2 4.8 %slice-start.5 = ((s8[6291456]{0:T(1024)(128)(4,1)}), s8[2097152]{0:T(1024)(128)(4,1)S(1)}, s32[]{:S(2)}) async-start(s8[6291456]{0:T(1024)(128)(4,1)} %bitcast.196), calls=%async_computation.6 | async-start | bytes 4194304
  155.2 4.8 %copy-start.10 = (bf16[12,16,32,128]{3,1,2,0:T(8,128)(2,1)S(1)}, bf16[12,16,32,128]{3,1,2,0:T(8,128)(2,1)}, u32[]{:S(2)}) copy-start(bf16[12,16,32,128]{3,1,2,0:T(8,128)(2,1)} %bitcast_convert_fusion.4) | copy-start | bytes 4718596
  155.2 6.6 %slice-start = ((s8[6291456]{0:T(1024)(128)(4,1)}), s8[4194304]{0:T(1024)(128)(4,1)S(1)}, s32[]{:S(2)}) async-start(s8[6291456]{0:T(1024)(128)(4,1)} %bitcast.192), calls=%async_computation.1 | async-start | bytes 8388608
  160.0 1.9 slice-start.1
  160.0 1.9 copy-start.5
  160.0 2.2 copy-start.8
  181.0 1.7 copy-start.3
  182.2 2.2 slice-start.10
  182.8 2.4 %slice-start.11 = ((s8[6291456]{0:T(1024)(128)(4,1)}), s8[2097152]{0:T(1024)(128)(4,1)S(1)}, s32[]{:S(2)}) async-start(s8[6291456]{0:T(1024)(128)(4,1)} %bitcast.202), calls=%async_computation.12 | async-start | bytes 4194304
  182.8 5.6 %slice-start.8 = ((s8[6291456]{0:T(1024)(128)(4,1)}), s8[4194304]{0:T(1024)(128)(4,1)S(1)}, s32[]{:S(2)}) async-start(s8[6291456]{0:T(1024)(128)(4,1)} %bitcast.200), calls=%async_computation.9 | async-start | bytes 8388608
  185.2 3.2 %slice-start.9 = ((s8[6291456]{0:T(1024)(128)(4,1)}), s8[2097152]{0:T(1024)(128)(4,1)S(1)}, s32[]{:S(2)}) async-start(s8[6291456]{0:T(1024)(128)(4,1)} %bitcast.200), calls=%async_computation.10 | async-start | bytes 4194304
  190.3 2.8 %slice-start.6 = ((s8[6291456]{0:T(1024)(128)(4,1)}), s8[4194304]{0:T(1024)(128)(4,1)S(1)}, s32[]{:S(2)}) async-start(s8[6291456]{0:T(1024)(128)(4,1)} %bitcast.198), calls=%async_computation.7 | async-start | bytes 8388608
  191.7 1.8 slice-start.7
  191.7 3.9 %slice-start.2 = ((s8[6291456]{0:T(1024)(128)(4,1)}), s8[4194304]{0:T(1024)(128)(4,1)S(1)}, s32[]{:S(2)}) async-start(s8[6291456]{0:T(1024)(128)(4,1)} %bitcast.194), calls=%async_computation.3 | async-start | bytes 8388608
  193.5 2.1 slice-start.3
Sparse Core Ops, SparseCore 0:
  9.7 39.4 all-gather.2
where the time goes:
time: 242 us; the launch traced here: 239 us
  waiting for transfers between devices  94.2 us (39%)
  matrix products  44 us (18%)
  blocking collectives  36.8 us (15%)
  local copies, waits for them, and re-layouts  35.7 us (15%)
  between operations  21.3 us (9%)
  starting transfers between devices  3.4 us (1%)
    ppermute x1, waiting for transfers between devices, from_behind(): lax.ppermute(value, axis, [(source, source + steps) for source in range(i...  59.1 us
    all_gather x1, waiting for transfers between devices, shards(): whole = lax.all_gather(own, 'sec', axis=0, tiled=True)  34.4 us
    psum x2, blocking collectives, shards(): lax.psum((squares, jnp.sum(xf * h), jnp.sum(xf * xf)), 'sec')  28.7 us
    dot_general x8, matrix products, apply_local(): jnp.einsum('qlxa,lqac->qxc', chosen, third, preferred_element_type=jnp.fl...  23.6 us
    gather x4, local copies, waits for them, and re-layouts, apply_local(): jnp.take(lenv[:, :, :, lo_row:lo_row + step_rows], left_row, axis=0)  21.6 us
    dot_general x8, matrix products, apply_local(): jnp.einsum('lwqp,pwac->lqac', mpo, first, preferred_element_type=jnp.floa...  14.6 us
    unnamed x1, blocking collectives  8.04 us
    slice x1, local copies, waits for them, and re-layouts, apply_local(): lenv[:, :, :, lo_row:lo_row + step_rows]  5.6 us
  transfers between devices with their start and end apart: 2, of which 2 were waited for; matrix products, arithmetic and copies ran while one was open for 7% of the time, Pallas kernels for 0%

commit v1 on v0

v1 whole, which is shorter than its diff:
```python
import functools

import jax
import jax.numpy as jnp
from jax import lax
from jax.experimental import pallas as pl
from jax.experimental.pallas import tpu as pltpu
from jax.sharding import PartitionSpec as P

ITERS = 2
CHUNKS = 3
MESH = pl.DeviceIdType.MESH
F32 = jnp.float32
BF16 = jnp.bfloat16


def dot(a, b):
    return jnp.dot(a, b, preferred_element_type=F32)


def iota(shape, dim):
    return lax.broadcasted_iota(jnp.int32, shape, dim)


def onehot(cond):
    return jnp.where(cond, 1.0, 0.0).astype(BF16)


def fold(values):
    return jnp.sum(values.reshape(-1, 8, values.shape[-1]), axis=0)


def whole_sum(tile):
    return jnp.sum(tile, axis=(0, 1), keepdims=True)


def order_block(env_ref, chunk):
    width = env_ref.shape[2]
    per = 8 if chunk < 2 else 4
    first = 0 if chunk < 2 else 8
    cols = 512
    start = chunk * cols if chunk < 2 else 0
    shift = 3 if chunk < 2 else 2
    block = jnp.concatenate([env_ref[first + bond] for bond in range(per)], axis=1)
    row = iota((per * width, cols), 0)
    col = iota((per * width, cols), 1) + start
    place = onehot((row >> 7 == (col & (per - 1))) & ((row & 127) == (col >> shift)))
    return dot(block, place).astype(BF16)


def build_mpo(left_ref, right_ref):
    n = 192
    row = iota((n, 1), 0)
    tail = row >= 128
    q = jnp.where(tail, (row - 128) >> 2, row >> 3)
    bond = jnp.where(tail, 8 + (row & 3), row & 7)
    col = iota((1, n), 1)
    pick = onehot(
        (iota((n, n), 0) >> 4 == iota((n, n), 1) >> 4) & ((iota((n, n), 0) & 3) == (iota((n, n), 1) & 3))
    )
    sixteen = iota((1, 16), 1)
    spread = dot(onehot(bond == sixteen), left_ref[...])
    spread = jnp.where(((col >> 2) & 3) == (q >> 2), spread, 0.0).astype(BF16)
    left = jnp.where(((col >> 2) & 3) == (q & 3), dot(spread, pick), 0.0).astype(BF16)
    spread = dot(onehot((row >> 4) == sixteen), right_ref[...])
    spread = jnp.where(((col >> 2) & 3) == ((row >> 2) & 3), spread, 0.0).astype(BF16)
    right = jnp.where(((col >> 2) & 3) == (row & 3), dot(spread, pick), 0.0).astype(BF16)
    return dot(left, right).astype(BF16)


def kernel(
    nseg, nsec,
    psi_ref, env_ref, renv_ref, left_ref, right_ref, charge_ref, rank_ref,
    state_ref, energy_ref, weight_ref,
    l0, l1, l2, own, x1, x3, mpo, flat, xt, xq, acc, sum_tx, sum_rx, share_tx, share_rx, run,
    shift_sem, up_sem, down_sem, side_sem, recv_sem, sum_send, sum_recv, share_send, share_recv,
):
    seg = lax.axis_index("seg")
    sec = lax.axis_index("sec")
    nz = nsec // 2
    z = sec // 2
    core = sec % 2
    slots = (l0, l1, l2)
    states, width = psi_ref.shape[0], psi_ref.shape[2]

    barrier = pltpu.get_barrier_semaphore()
    for d in range(1, nsec):
        pl.semaphore_signal(barrier, inc=1, device_id=(seg, lax.rem(sec + d, nsec)), device_id_type=MESH)
    for d in range(1, nseg):
        pl.semaphore_signal(barrier, inc=1, device_id=(lax.rem(seg + d, nseg), sec), device_id_type=MESH)

    def copy(src, dst, send, recv, to):
        return pltpu.make_async_remote_copy(
            src_ref=src, dst_ref=dst, send_sem=send, recv_sem=recv, device_id=to, device_id_type=MESH
        )

    def shift(c):
        return copy(own.at[c], slots[c].at[sec], shift_sem.at[c], recv_sem.at[c, sec], (seg + 1, sec))

    def up(c, h):
        s = sec - 2 * h
        return copy(slots[c].at[s], slots[c].at[s], up_sem.at[c, h], recv_sem.at[c, s], (seg, sec + 2))

    def down(c, h):
        s = sec + 2 * h
        return copy(slots[c].at[s], slots[c].at[s], down_sem.at[c, h], recv_sem.at[c, s], (seg, sec - 2))

    def side(c, s):
        return copy(
            slots[c].at[s], slots[c].at[s], side_sem.at[c, s // 2], recv_sem.at[c, s], (seg, sec + 1 - 2 * core)
        )

    def arrived(c, s):
        copy(slots[c].at[s], slots[c].at[s], side_sem.at[c, 0], recv_sem.at[c, s], (seg, sec)).wait_recv()

    def order(c):
        block = order_block(env_ref, c)
        own[c] = block

        @pl.when(seg == 0)
        def _():
            slots[c][sec] = block

    def shift_out(c):
        @pl.when(seg < nseg - 1)
        def _():
            shift(c).start()

    def hop(c, h):
        if h == 0:
            @pl.when(seg > 0)
            def _():
                arrived(c, sec)

            @pl.when(z < nz - 1)
            def _():
                up(c, 0).start()

            @pl.when(z > 0)
            def _():
                down(c, 0).start()

            side(c, sec).start()
            return

        @pl.when(z >= h)
        def _():
            arrived(c, sec - 2 * h)

            @pl.when(z < nz - 1)
            def _():
                up(c, h).start()

            side(c, sec - 2 * h).start()

        @pl.when(z + h < nz)
        def _():
            arrived(c, sec + 2 * h)

            @pl.when(z > 0)
            def _():
                down(c, h).start()

            side(c, sec + 2 * h).start()

    def settle(c):
        for k in range(nz):
            arrived(c, 2 * k + 1 - core)

    def drain():
        for c in range(CHUNKS):
            @pl.when(seg < nseg - 1)
            def _():
                shift(c).wait_send()

            for h in range(nz):
                @pl.when((z >= h) & (z < nz - 1))
                def _():
                    up(c, h).wait_send()

                @pl.when((z + h < nz) & (z > 0))
                def _():
                    down(c, h).wait_send()

                side(c, 2 * h + core).wait_send()

    def flatten(first):
        if first:
            for p in range(states):
                value = psi_ref[p].astype(F32)
                flat[pl.ds(p, width, stride=states), :] = value
        xt[...] = flat[...].astype(BF16)

    def right_apply(w_lo, w_hi):
        def one(w, carry):
            rhs = jnp.concatenate([renv_ref[2 * w], renv_ref[2 * w + 1]], axis=1)
            rows = 512
            for block in range(states * width // rows):
                out = dot(xt[block * rows : (block + 1) * rows, :], rhs).astype(BF16)
                lo = block * rows // states
                for half in range(2):
                    x1[pl.ds(lo, rows // states), pl.ds(pl.multiple_of((2 * w + half) * states, states), states), :] = (
                        out[:, half * width : (half + 1) * width].reshape(rows // states, states, width)
                    )
            return carry

        lax.fori_loop(w_lo, w_hi, one, 0)

    def mpo_apply(lo, hi):
        group = 8
        low = iota((states // 2, 8, width), 1) < 4

        def one(step, carry):
            operator = mpo[...]
            for quad in range(group // 4):
                a = step * group + quad * 4
                tails = []
                for pair in range(2):
                    at = a + 2 * pair
                    rhs = jnp.concatenate([x1[at], x1[at + 1]], axis=1)
                    out = dot(operator, rhs)
                    parts = [out[:, :width], out[:, width:]]
                    heads = [part[:128].reshape(states, 8, width) for part in parts]
                    x3[:, pl.ds(pl.multiple_of(at * 8, 16), 16), :] = jnp.concatenate(heads, axis=1).astype(BF16)
                    a_tail, b_tail = [part[128:].reshape(states // 2, 8, width) for part in parts]
                    even = jnp.where(low, a_tail, pltpu.roll(b_tail, 4, 1))
                    odd = jnp.where(low, pltpu.roll(a_tail, 4, 1), b_tail)
                    tails.append((even, odd))
                even = jnp.concatenate([tails[0][0], tails[1][0]], axis=1).astype(BF16)
                odd = jnp.concatenate([tails[0][1], tails[1][1]], axis=1).astype(BF16)
                both = jnp.stack([even, odd], axis=1).reshape(states, 16, width)
                x3[:, pl.ds(pl.multiple_of(1024 + a * 4, 16), 16), :] = both
            return carry

        lax.fori_loop(lo, hi, one, 0)

    def left_of(q):
        return lax.rem(sec - charge_ref[q] + nsec, nsec)

    keep = iota((width, width), 1) < rank_ref[0]
    per = 4
    zero = jnp.zeros((8, width), F32)

    def left_apply(q, chunks):
        s = left_of(q)
        total = None
        for c in chunks:
            term = dot(slots[c][s], x3[q, c * 512 : (c + 1) * 512, :])
            total = term if total is None else total + term
        return total

    def partial(c):
        def some(step, carry):
            for j in range(per):
                q = step * per + j
                term = left_apply(q, (c,))
                acc[q] = term if c == 0 else acc[q] + term
            return carry

        lax.fori_loop(0, states // per, some, 0)

    def exchange(step):
        for d in range(1, nsec):
            copy(
                sum_tx.at[step], sum_rx.at[step, sec], sum_send.at[step, d], sum_recv.at[step, sec],
                (seg, lax.rem(sec + d, nsec)),
            ).start()

    def collect(step):
        for d in range(1, nsec):
            other = lax.rem(sec + d, nsec)
            copy(
                sum_tx.at[step], sum_rx.at[step, other], sum_send.at[step, d], sum_recv.at[step, other], (seg, other)
            ).wait_recv()
        total = sum_rx[step, 0]
        for other in range(1, nsec):
            total = total + sum_rx[step, other]
        return total

    run[...] = jnp.zeros_like(run)
    order(0)
    pl.semaphore_wait(barrier, nsec + nseg - 2)
    shift_out(0)
    order(1)
    shift_out(1)
    order(2)
    shift_out(2)
    mpo[...] = build_mpo(left_ref, right_ref)
    hop(0, 0)
    flatten(True)
    pairs = renv_ref.shape[0] // 2
    right_apply(0, pairs // 2)
    hop(1, 0)
    right_apply(pairs // 2, pairs)
    hop(2, 0)
    hop(0, 1)
    steps = width // 8
    mpo_apply(0, steps // 2)
    hop(1, 1)
    mpo_apply(steps // 2, steps)
    hop(2, 1)
    for h in range(2, nz):
        for c in range(CHUNKS):
            hop(c, h)
            if h == nz - 1 and c < 2:
                settle(c)
                partial(c)
    settle(2)

    def first(step, squares):
        for j in range(per):
            q = step * per + j
            h = acc[q] + left_apply(q, (2,))
            u = jnp.where(keep, psi_ref[q].astype(F32) - 0.5 * h, 0.0)
            flat[pl.ds(q, width, stride=states), :] = u
            xq[q] = u.astype(BF16)
            squares = squares + fold(u * u)
        return squares

    squares = lax.fori_loop(0, states // per, first, zero)
    sum_tx[0] = jnp.stack([squares, zero, zero])
    sum_rx[0, sec] = jnp.stack([squares, zero, zero])
    exchange(0)
    flatten(False)
    right_apply(0, pairs)
    mpo_apply(0, steps)
    count = float(nsec * states * width * width)
    total = collect(0)
    scale = lax.rsqrt(whole_sum(total[0]) / count + 1e-06)

    def last(step, carry):
        squares, inner, own_sum = carry
        for j in range(per):
            q = step * per + j
            h = left_apply(q, (0, 1, 2)) * scale
            x = xq[q].astype(F32) * scale
            u = jnp.where(keep, x - 0.5 * h, 0.0)
            acc[q] = u
            squares = squares + fold(u * u)
            inner = inner + fold(x * h)
            own_sum = own_sum + fold(x * x)
        return squares, inner, own_sum

    sums = lax.fori_loop(0, states // per, last, (zero, zero, zero))
    sum_tx[1] = jnp.stack(sums)
    sum_rx[1, sec] = jnp.stack(sums)
    exchange(1)
    mine = whole_sum(sums[0])
    total = collect(1)
    all_squares = whole_sum(total[0])
    share = jnp.log(float(nsec) * mine / all_squares)
    share_tx[...] = jnp.broadcast_to(share, share_tx.shape)

    def share_copy(d, back):
        there = seg - d if back else seg + d
        slot = share_rx.at[there if back else seg]
        sem = share_recv.at[there if back else seg]
        return copy(share_tx, slot, share_send.at[d], sem, (there, sec))

    for d in range(1, nseg):
        @pl.when(seg + d < nseg)
        def _():
            share_copy(d, False).start()

    scale = lax.rsqrt(all_squares / count + 1e-06)
    energy_ref[...] = whole_sum(total[1]) / whole_sum(total[2])

    def write(q, carry):
        state_ref[q] = (acc[q] * scale).astype(BF16)
        return carry

    lax.fori_loop(0, states, write, 0)
    run[...] = share_tx[...]
    for d in range(1, nseg):
        @pl.when(seg - d >= 0)
        def _():
            share_copy(d, True).wait_recv()
            run[...] += share_rx[seg - d]

    weight_ref[...] = run[0:1, 0:1]
    drain()
    for step in range(ITERS):
        for d in range(1, nsec):
            copy(
                sum_tx.at[step], sum_rx.at[step, sec], sum_send.at[step, d], sum_recv.at[step, sec],
                (seg, lax.rem(sec + d, nsec)),
            ).wait_send()
    for d in range(1, nseg):
        @pl.when(seg + d < nseg)
        def _():
            share_copy(d, False).wait_send()


def shards(psi, env_build, env_right, site_left, site_right, charge, rank):
    nseg, nsec = lax.axis_size("seg"), lax.axis_size("sec")
    x = psi[0, 0]
    states, width = x.shape[0], x.shape[2]
    bonds = env_build.shape[2]
    left = jnp.pad(site_left.reshape(bonds, -1), ((0, 16 - bonds), (0, 0)))
    right = jnp.pad(site_right.reshape(bonds, -1), ((0, 16 - bonds), (0, 0)))
    vmem = pl.BlockSpec(memory_space=pltpu.VMEM)
    smem = pl.BlockSpec(memory_space=pltpu.SMEM)
    dma = pltpu.SemaphoreType.DMA
    nz = nsec // 2
    slot = pltpu.VMEM((nsec, width, 512), BF16)
    state, energy, weight = pl.pallas_call(
        functools.partial(kernel, nseg, nsec),
        out_shape=(
            jax.ShapeDtypeStruct(x.shape, BF16),
            jax.ShapeDtypeStruct((1, 1), F32),
            jax.ShapeDtypeStruct((1, 1), F32),
        ),
        in_specs=[vmem] * 5 + [smem] * 2,
        out_specs=(vmem, vmem, vmem),
        scratch_shapes=[
            slot, slot, slot,
            pltpu.VMEM((CHUNKS, width, 512), BF16),
            pltpu.VMEM((width, bonds * states, width), BF16),
            pltpu.VMEM((states, bonds * width, width), BF16),
            pltpu.VMEM((bonds * states, bonds * states), BF16),
            pltpu.VMEM((states * width, width), F32),
            pltpu.VMEM((states * width, width), BF16),
            pltpu.VMEM((states, width, width), BF16),
            pltpu.VMEM((states, width, width), F32),
            pltpu.VMEM((ITERS, 3, 8, width), F32),
            pltpu.VMEM((ITERS, nsec, 3, 8, width), F32),
            pltpu.VMEM((8, width), F32),
            pltpu.VMEM((nseg, 8, width), F32),
            pltpu.VMEM((8, width), F32),
            dma((CHUNKS,)),
            dma((CHUNKS, nz)),
            dma((CHUNKS, nz)),
            dma((CHUNKS, nz)),
            dma((CHUNKS, nsec)),
            dma((ITERS, nsec)),
            dma((ITERS, nsec)),
            dma((nseg,)),
            dma((nseg,)),
        ],
        compiler_params=pltpu.CompilerParams(
            collective_id=0, has_side_effects=True, vmem_limit_bytes=52 * 2**20
        ),
    )(x, env_build[0, 0], env_right[0, 0], left, right, charge, rank)
    return (state[None, None], energy.reshape(1), weight.reshape(1, 1))


def solution(mesh):
    return jax.shard_map(
        shards,
        mesh=mesh,
        in_specs=(
            P("seg", "sec", None, None, None),
            P("seg", "sec", None, None, None),
            P("seg", "sec", None, None, None),
            P(),
            P(),
            P(),
            P("sec"),
        ),
        out_specs=(P("seg", "sec", None, None, None), P("seg"), P("seg", "sec")),
        check_vma=False,
    )
```

time: 242 us -> 69.5 us (0.29); the launches traced: 239 us -> 69.1 us
  waiting for transfers between devices: 94.2 us -> 0 us
  Pallas kernels: 0 us -> 57.6 us
  matrix products: 44 us -> 0 us
  blocking collectives: 36.8 us -> 0 us
  local copies, waits for them, and re-layouts: 35.7 us -> 6.62 us
  between operations: 21.3 us -> 4.82 us
  starting transfers between devices: 3.4 us -> 0 us
    ppermute x1 -> x0, waiting for transfers between devices: 59.1 us -> none  [from_behind(): lax.ppermute(value, axis, [(source, source + steps) for source in range(i...]
    pallas_call x0 -> x1, Pallas kernels: none -> 57.6 us  [shards(): pl.pallas_call(functools.partial(kernel, nseg, nsec), out_shape=(jax.Shap...]
    dot_general x25 -> x0, matrix products: 44 us -> none  [the longest x8 23.6 us: apply_local(): jnp.einsum('qlxa,lqac->qxc', chosen, third, preferred_element_type=jnp.fl...]
    all_gather x1 -> x0, waiting for transfers between devices: 34.4 us -> none  [shards(): whole = lax.all_gather(own, 'sec', axis=0, tiled=True)]
    psum x2 -> x0, blocking collectives: 28.7 us -> none  [shards(): lax.psum((squares, jnp.sum(xf * h), jnp.sum(xf * xf)), 'sec')]
    gather x4 -> x0, local copies, waits for them, and re-layouts: 21.6 us -> none  [apply_local(): jnp.take(lenv[:, :, :, lo_row:lo_row + step_rows], left_row, axis=0)]
    unnamed x1 -> x0, blocking collectives: 8.04 us -> none
    slice x1 -> x0, local copies, waits for them, and re-layouts: 5.6 us -> none  [apply_local(): lenv[:, :, :, lo_row:lo_row + step_rows]]
  transfers between devices with their start and end apart: 2 -> 0, of which waited for: 2 -> 0; matrix products, arithmetic and copies ran while one was open for 7% -> 0% of each run, Pallas kernels for 0% -> 0%
where the time goes in v1:
time: 69.5 us; the launch traced here: 69.1 us
  Pallas kernels  57.6 us (83%)
  local copies, waits for them, and re-layouts  6.62 us (10%)
  between operations  4.82 us (7%)
    pallas_call x1, Pallas kernels, shards(): pl.pallas_call(functools.partial(kernel, nseg, nsec), out_shape=(jax.Shap...  57.6 us
    unnamed x13, local copies, waits for them, and re-layouts  6.42 us

profile of v1, /device:TPU:4, one launch (start us, length us, event | category | flops | bytes accessed | tf_op | source)
XLA Modules:
  0.0 69.1 jit_solution(11482880380857854446)
XLA Ops:
  1.3 1.0 %copy.12 = bf16[12,12,4,4]{0,3,2,1:T(4,128)(2,1)S(1)} copy(bf16[12,12,4,4]{1,3,2,0:T(4,128)(2,1)} %param.10) | data formatting | bytes 9216 | tf_op args[3]
  2.3 0.0 copy-start.4
  2.3 0.1 copy.13
  2.4 0.7 copy-done.4
  3.1 0.2 copy.14
  3.3 0.1 copy.15
  3.4 0.0 copy-start.3
  3.4 0.6 copy-done.3
  4.1 0.0 copy-start
  4.1 1.0 %copy-done = bf16[1,1,16,128,128]{4,3,2,1,0:T(8,128)(2,1)S(1)} copy-done((bf16[1,1,16,128,128]{4,3,2,1,0:T(8,128)(2,1)S(1)}, bf16[1,1,16,128,128]{4,3,2,1,0:T(8,128)(2,1)}, u32[]{:S(2)}) %copy-start) | copy-done | bytes 524312
  5.1 0.0 copy-start.1
  5.1 1.0 %copy-done.1 = bf16[1,1,12,128,128]{4,3,2,1,0:T(8,128)(2,1)S(1)} copy-done((bf16[1,1,12,128,128]{4,3,2,1,0:T(8,128)(2,1)S(1)}, bf16[1,1,12,128,128]{4,3,2,1,0:T(8,128)(2,1)}, u32[]{:S(2)}) %copy-start.1) | copy-done | bytes 393240
  6.1 0.0 copy-start.2
  6.1 1.0 %copy-done.2 = bf16[1,1,12,128,128]{4,3,2,1,0:T(8,128)(2,1)S(1)} copy-done((bf16[1,1,12,128,128]{4,3,2,1,0:T(8,128)(2,1)S(1)}, bf16[1,1,12,128,128]{4,3,2,1,0:T(8,128)(2,1)}, u32[]{:S(2)}) %copy-start.2) | copy-done | bytes 393240
  7.1 57.6 %shard_map.94 = (bf16[16,128,128]{2,1,0:T(8,128)(2,1)S(1)}, f32[1,1]{1,0:T(1,128)}, f32[1,1]{1,0:T(1,128)}) custom-call(bf16[16,128,128]{2,1,0:T(8,128)(2,1)S(1)} %bitcast.7, bf16[12,128,128]{2,1,0:T(8,128)(2,1)S(1)} %bitcast.9, bf16[12,128,128]{2,1,0:T(8,128)(2,1)S(1)} %bitcast.10, bf16[16,192]{1,0:T(8,128)(2,1)S(1)} %pad.7.left_ref, ...), custom_call_target="tpu_custom_call" | custom-call | tf_op jit(solution)/shard_map/pallas_call | solution.py:406
  64.8 0.8 %copy.20 = bf16[1,1,16,128,128]{4,3,2,1,0:T(8,128)(2,1)} copy(bf16[1,1,16,128,128]{4,3,2,1,0:T(8,128)(2,1)S(1)} %bitcast.8) | data formatting | bytes 1048576
  (2 shorter events, 0.0 us)
Async XLA Ops:
  2.3 0.8 %copy-start.4 = (bf16[12,12,4,4]{1,3,2,0:T(4,128)(2,1)S(1)}, bf16[12,12,4,4]{1,3,2,0:T(4,128)(2,1)}, u32[]{:S(2)}) copy-start(bf16[12,12,4,4]{1,3,2,0:T(4,128)(2,1)} %param.11) | copy-start | bytes 13828
  3.4 0.7 copy-start.3
  4.1 1.0 %copy-start = (bf16[1,1,16,128,128]{4,3,2,1,0:T(8,128)(2,1)S(1)}, bf16[1,1,16,128,128]{4,3,2,1,0:T(8,128)(2,1)}, u32[]{:S(2)}) copy-start(bf16[1,1,16,128,128]{4,3,2,1,0:T(8,128)(2,1)} %param.7) | copy-start | bytes 1572868
  5.1 1.0 %copy-start.1 = (bf16[1,1,12,128,128]{4,3,2,1,0:T(8,128)(2,1)S(1)}, bf16[1,1,12,128,128]{4,3,2,1,0:T(8,128)(2,1)}, u32[]{:S(2)}) copy-start(bf16[1,1,12,128,128]{4,3,2,1,0:T(8,128)(2,1)} %param.8) | copy-start | bytes 1179652
  6.1 1.0 %copy-start.2 = (bf16[1,1,12,128,128]{4,3,2,1,0:T(8,128)(2,1)S(1)}, bf16[1,1,12,128,128]{4,3,2,1,0:T(8,128)(2,1)}, u32[]{:S(2)}) copy-start(bf16[1,1,12,128,128]{4,3,2,1,0:T(8,128)(2,1)} %param.9) | copy-start | bytes 1179652

commit v2 on v1

v2 whole, which is shorter than its diff:
```python
import functools

import jax
import jax.numpy as jnp
from jax import lax
from jax.experimental import pallas as pl
from jax.experimental.pallas import tpu as pltpu
from jax.sharding import PartitionSpec as P

ITERS = 2
CHUNKS = 4
MESH = pl.DeviceIdType.MESH
F32 = jnp.float32
BF16 = jnp.bfloat16


def dot(a, b):
    return jnp.dot(a, b, preferred_element_type=F32)


def iota(shape, dim):
    return lax.broadcasted_iota(jnp.int32, shape, dim)


def onehot(cond):
    return jnp.where(cond, 1.0, 0.0).astype(BF16)


def fold(values):
    return jnp.sum(values.reshape(-1, 8, values.shape[-1]), axis=0)


def whole_sum(tile):
    return jnp.sum(tile, axis=(0, 1), keepdims=True)


def order_rows(env_ref, lo, rows):
    width = env_ref.shape[2]
    lane = iota((rows, width), 1)
    blocks = []
    for first, per in ((0, 8), (8, 4)):
        parts = [env_ref[first + bond, lo : lo + rows, :].astype(F32) for bond in range(per)]
        for j in range(per):
            block = parts[0] if j == 0 else pltpu.roll(parts[0], width - j, 1)
            for bond in range(1, per):
                turned = parts[bond] if bond == j else pltpu.roll(parts[bond], (bond - j) % width, 1)
                block = jnp.where((lane & (per - 1)) == bond, turned, block)
            blocks.append(block.astype(BF16))
    return blocks


def stage_sites(site_ref, stage):
    stage[...] = jnp.zeros_like(stage)
    local = site_ref.shape[1]
    bonds = site_ref.shape[3]

    def one(bond, carry):
        for new in range(local):
            stage[pl.ds(bond * local * local + new * local, local), 0:bonds] = site_ref[bond, new].astype(F32)
        return carry

    lax.fori_loop(0, site_ref.shape[0], one, 0)


def build_mpo(left_ref, right_ref, stage):
    n = 192
    row = iota((n, 1), 0)
    tail = row >= 128
    q = jnp.where(tail, (row - 128) >> 2, row >> 3)
    bond = jnp.where(tail, 8 + (row & 3), row & 7)
    col = iota((1, n), 1)
    spread = onehot(iota((stage.shape[1], n), 0) == (iota((stage.shape[1], n), 1) >> 4))
    stage_sites(left_ref, stage)
    value = dot(stage[...].astype(BF16), spread)
    value = jnp.where((row & 3) == (col & 3), value, 0.0).astype(BF16)
    value = dot(onehot((bond == (col >> 4)) & ((q >> 2) == ((col >> 2) & 3))), value)
    left = jnp.where((q & 3) == ((col >> 2) & 3), value, 0.0).astype(BF16)
    stage_sites(right_ref, stage)
    value = dot(stage[...].astype(BF16), spread)
    value = jnp.where((row & 3) == (col & 3), value, 0.0).astype(BF16)
    value = dot(onehot(((row >> 4) == (col >> 4)) & (((row >> 2) & 3) == ((col >> 2) & 3))), value)
    right = jnp.where((row & 3) == ((col >> 2) & 3), value, 0.0).astype(BF16)
    return dot(left, right).astype(BF16)


def kernel(
    nseg, nsec,
    psi_hbm, env_hbm, renv_hbm, left_hbm, right_hbm, charge_hbm, rank_hbm,
    state_ref, energy_ref, weight_ref,
    l0, l1, l2, l3, own, psi_ref, env_ref, renv_ref, left_ref, right_ref, charge_ref, rank_ref, x1, x3a, x3b, mpo, stage, flat, xt, xq, acc,
    sum_tx, sum_rx, share_tx, share_rx, run,
    load_sem, shift_sem, up_sem, down_sem, side_sem, recv_sem, sum_send, sum_recv, share_send, share_recv,
):
    seg = lax.axis_index("seg")
    sec = lax.axis_index("sec")
    nz = nsec // 2
    z = sec // 2
    core = sec % 2
    slots = (l0, l1, l2, l3)
    states, width = psi_ref.shape[0], psi_ref.shape[2]
    rows = width // CHUNKS

    pairs = (
        (env_hbm, env_ref), (psi_hbm, psi_ref), (renv_hbm, renv_ref), (left_hbm, left_ref), (right_hbm, right_ref),
        (charge_hbm, charge_ref), (rank_hbm, rank_ref),
    )
    loads = [
        pltpu.make_async_copy(src, dst, load_sem.at[i])
        for i, (src, dst) in enumerate(pairs)
    ]
    for load in loads:
        load.start()

    barrier = pltpu.get_barrier_semaphore()
    for d in range(1, nsec):
        pl.semaphore_signal(barrier, inc=1, device_id=(seg, lax.rem(sec + d, nsec)), device_id_type=MESH)
    for d in range(1, nseg):
        pl.semaphore_signal(barrier, inc=1, device_id=(lax.rem(seg + d, nseg), sec), device_id_type=MESH)

    def copy(src, dst, send, recv, to):
        return pltpu.make_async_remote_copy(
            src_ref=src, dst_ref=dst, send_sem=send, recv_sem=recv, device_id=to, device_id_type=MESH
        )

    def shift(c):
        return copy(own.at[c], slots[c].at[sec], shift_sem.at[c], recv_sem.at[c, sec], (seg + 1, sec))

    def up(c, h):
        s = sec - 2 * h
        return copy(slots[c].at[s], slots[c].at[s], up_sem.at[c, h], recv_sem.at[c, s], (seg, sec + 2))

    def down(c, h):
        s = sec + 2 * h
        return copy(slots[c].at[s], slots[c].at[s], down_sem.at[c, h], recv_sem.at[c, s], (seg, sec - 2))

    def side(c, s):
        return copy(
            slots[c].at[s], slots[c].at[s], side_sem.at[c, s // 2], recv_sem.at[c, s], (seg, sec + 1 - 2 * core)
        )

    def arrived(c, s):
        copy(slots[c].at[s], slots[c].at[s], side_sem.at[c, 0], recv_sem.at[c, s], (seg, sec)).wait_recv()

    def order(c):
        for j, block in enumerate(order_rows(env_ref, c * rows, rows)):
            own[c, :, j * width : (j + 1) * width] = block

        @pl.when(seg == 0)
        def _():
            slots[c][sec] = own[c]

    def shift_out(c):
        @pl.when(seg < nseg - 1)
        def _():
            shift(c).start()

    def hop(c, h):
        if h == 0:
            @pl.when(seg > 0)
            def _():
                arrived(c, sec)

            @pl.when(z < nz - 1)
            def _():
                up(c, 0).start()

            @pl.when(z > 0)
            def _():
                down(c, 0).start()

            side(c, sec).start()
            return

        @pl.when(z >= h)
        def _():
            arrived(c, sec - 2 * h)

            @pl.when(z < nz - 1)
            def _():
                up(c, h).start()

            side(c, sec - 2 * h).start()

        @pl.when(z + h < nz)
        def _():
            arrived(c, sec + 2 * h)

            @pl.when(z > 0)
            def _():
                down(c, h).start()

            side(c, sec + 2 * h).start()

    def settle(c):
        for k in range(nz):
            arrived(c, 2 * k + 1 - core)

    def drain():
        for c in range(CHUNKS):
            @pl.when(seg < nseg - 1)
            def _():
                shift(c).wait_send()

            for h in range(nz):
                @pl.when((z >= h) & (z < nz - 1))
                def _():
                    up(c, h).wait_send()

                @pl.when((z + h < nz) & (z > 0))
                def _():
                    down(c, h).wait_send()

                side(c, 2 * h + core).wait_send()

    def flatten(c):
        for p in range(states):
            flat[pl.ds(p, rows, stride=states), :] = psi_ref[p, c * rows : (c + 1) * rows, :].astype(F32)

    def right_apply():
        xt[...] = flat[...].astype(BF16)

        def one(w, carry):
            rhs = jnp.concatenate([renv_ref[2 * w], renv_ref[2 * w + 1]], axis=1)
            out = dot(xt[...], rhs).astype(BF16)
            for half in range(2):
                x1[:, pl.ds(pl.multiple_of((2 * w + half) * states, states), states), :] = (
                    out[:, half * width : (half + 1) * width].reshape(rows, states, width)
                )
            return carry

        lax.fori_loop(0, renv_ref.shape[0] // 2, one, 0)

    def mpo_apply(c, x3):
        group = 16
        low = iota((states // 2, 8, width), 1) < 4

        def one(step, carry):
            operator = mpo[...]
            a = step * group
            at = pl.multiple_of(c * rows + a, group)

            def pair(j):
                out = dot(operator, jnp.concatenate([x1[a + j], x1[a + j + 8]], axis=1))
                parts = [out[:, :width], out[:, width:]]
                heads = [part[:128].reshape(states, 8, width) for part in parts]
                x3[:, pl.ds(pl.multiple_of(j * width + at, 16), 16), :] = jnp.concatenate(heads, axis=1).astype(BF16)
                return [part[128:].reshape(states // 2, 8, width) for part in parts]

            for j in range(4):
                evens, odds = [], []
                for a_tail, b_tail in zip(pair(j), pair(j + 4)):
                    evens.append(jnp.where(low, a_tail, pltpu.roll(b_tail, 4, 1)))
                    odds.append(jnp.where(low, pltpu.roll(a_tail, 4, 1), b_tail))
                even = jnp.concatenate(evens, axis=1).astype(BF16)
                odd = jnp.concatenate(odds, axis=1).astype(BF16)
                both = jnp.stack([even, odd], axis=1).reshape(states, 16, width)
                x3[:, pl.ds(pl.multiple_of((8 + j) * width + at, 16), 16), :] = both
            return carry

        lax.fori_loop(0, rows // group, one, 0)

    def left_of(q):
        return lax.rem(sec - charge_ref[q] + nsec, nsec)

    per = 4
    zero = jnp.zeros((8, width), F32)

    def first(c, squares, keep):
        def some(step, squares):
            for j in range(per):
                q = step * per + j
                h = dot(slots[c][left_of(q)], x3a[q])
                u = jnp.where(keep, psi_ref[q, c * rows : (c + 1) * rows, :].astype(F32) - 0.5 * h, 0.0)
                flat[pl.ds(q, rows, stride=states), :] = u
                xq[q, c * rows : (c + 1) * rows, :] = u.astype(BF16)
                squares = squares + fold(u * u)
            return squares

        return lax.fori_loop(0, states // per, some, squares)

    def exchange(step):
        for d in range(1, nsec):
            copy(
                sum_tx.at[step], sum_rx.at[step, sec], sum_send.at[step, d], sum_recv.at[step, sec],
                (seg, lax.rem(sec + d, nsec)),
            ).start()

    def collect(step):
        for d in range(1, nsec):
            other = lax.rem(sec + d, nsec)
            copy(
                sum_tx.at[step], sum_rx.at[step, other], sum_send.at[step, d], sum_recv.at[step, other], (seg, other)
            ).wait_recv()
        total = sum_rx[step, 0]
        for other in range(1, nsec):
            total = total + sum_rx[step, other]
        return total

    loads[0].wait()
    order(0)
    pl.semaphore_wait(barrier, nsec + nseg - 2)
    shift_out(0)
    for c in range(1, CHUNKS):
        order(c)
        shift_out(c)
    for load in loads[1:]:
        load.wait()
    mpo[...] = build_mpo(left_ref, right_ref, stage)
    keep = iota((rows, width), 1) < rank_ref[0]
    squares = zero
    for t in range(CHUNKS + nz - 1):
        for c in reversed(range(CHUNKS)):
            if 0 <= t - c < nz:
                hop(c, t - c)
        if t < CHUNKS:
            flatten(t)
            right_apply()
            mpo_apply(t, x3a)
        c = t - nz + 1
        if c >= 0:
            settle(c)
            squares = first(c, squares, keep)
            if c == CHUNKS - 1:
                sums = jnp.stack([squares, zero, zero])
                sum_tx[0] = sums
                sum_rx[0, sec] = sums
                exchange(0)
            right_apply()
            mpo_apply(c, x3b)

    count = float(nsec * states * width * width)
    total = collect(0)
    scale = lax.rsqrt(whole_sum(total[0]) / count + 1e-06)

    keep_all = iota((width, width), 1) < rank_ref[0]

    def last(step, carry):
        squares, inner, own_sum = carry
        for j in range(per):
            q = step * per + j
            s = left_of(q)
            h = dot(jnp.concatenate([slot[s] for slot in slots], axis=0), x3b[q]) * scale
            x = xq[q].astype(F32) * scale
            u = jnp.where(keep_all, x - 0.5 * h, 0.0)
            acc[q] = u
            squares = squares + fold(u * u)
            inner = inner + fold(x * h)
            own_sum = own_sum + fold(x * x)
        return squares, inner, own_sum

    sums = lax.fori_loop(0, states // per, last, (zero, zero, zero))
    sum_tx[1] = jnp.stack(sums)
    sum_rx[1, sec] = jnp.stack(sums)
    exchange(1)
    mine = whole_sum(sums[0])
    total = collect(1)
    all_squares = whole_sum(total[0])
    share = jnp.log(float(nsec) * mine / all_squares)
    share_tx[...] = jnp.broadcast_to(share, share_tx.shape)

    def share_copy(d, back):
        there = seg - d if back else seg + d
        slot = share_rx.at[there if back else seg]
        sem = share_recv.at[there if back else seg]
        return copy(share_tx, slot, share_send.at[d], sem, (there, sec))

    for d in range(1, nseg):
        @pl.when(seg + d < nseg)
        def _():
            share_copy(d, False).start()

    scale = lax.rsqrt(all_squares / count + 1e-06)
    energy_ref[...] = whole_sum(total[1]) / whole_sum(total[2])

    def write(q, carry):
        state_ref[q] = (acc[q] * scale).astype(BF16)
        return carry

    lax.fori_loop(0, states, write, 0)
    run[...] = share_tx[...]
    for d in range(1, nseg):
        @pl.when(seg - d >= 0)
        def _():
            share_copy(d, True).wait_recv()
            run[...] += share_rx[seg - d]

    weight_ref[...] = run[0:1, 0:1]
    drain()
    for step in range(ITERS):
        for d in range(1, nsec):
            copy(
                sum_tx.at[step], sum_rx.at[step, sec], sum_send.at[step, d], sum_recv.at[step, sec],
                (seg, lax.rem(sec + d, nsec)),
            ).wait_send()
    for d in range(1, nseg):
        @pl.when(seg + d < nseg)
        def _():
            share_copy(d, False).wait_send()


def shards(psi, env_build, env_right, site_left, site_right, charge, rank):
    nseg, nsec = lax.axis_size("seg"), lax.axis_size("sec")
    x = psi[0, 0]
    states, width = x.shape[0], x.shape[2]
    bonds = env_build.shape[2]
    left = site_left.transpose(0, 2, 3, 1)
    right = site_right.transpose(0, 2, 3, 1)
    hbm = pl.BlockSpec(memory_space=pltpu.HBM)
    vmem = pl.BlockSpec(memory_space=pltpu.VMEM)
    dma = pltpu.SemaphoreType.DMA
    nz = nsec // 2
    rows = width // CHUNKS
    slot = pltpu.VMEM((nsec, rows, bonds * width), BF16)
    state, energy, weight = pl.pallas_call(
        functools.partial(kernel, nseg, nsec),
        out_shape=(
            jax.ShapeDtypeStruct(x.shape, BF16),
            jax.ShapeDtypeStruct((1, 1), F32),
            jax.ShapeDtypeStruct((1, 1), F32),
        ),
        in_specs=[hbm] * 7,
        out_specs=(vmem, vmem, vmem),
        scratch_shapes=[
            slot, slot, slot, slot,
            pltpu.VMEM((CHUNKS, rows, bonds * width), BF16),
            pltpu.VMEM(x.shape, BF16),
            pltpu.VMEM((bonds, width, width), BF16),
            pltpu.VMEM((bonds, width, width), BF16),
            pltpu.VMEM(left.shape, BF16),
            pltpu.VMEM(right.shape, BF16),
            pltpu.SMEM(charge.shape, jnp.int32),
            pltpu.SMEM(rank.shape, jnp.int32),
            pltpu.VMEM((rows, bonds * states, width), BF16),
            pltpu.VMEM((states, bonds * width, width), BF16),
            pltpu.VMEM((states, bonds * width, width), BF16),
            pltpu.VMEM((bonds * states, bonds * states), BF16),
            pltpu.VMEM((bonds * states, 128), F32),
            pltpu.VMEM((states * rows, width), F32),
            pltpu.VMEM((states * rows, width), BF16),
            pltpu.VMEM((states, width, width), BF16),
            pltpu.VMEM((states, width, width), F32),
            pltpu.VMEM((ITERS, 3, 8, width), F32),
            pltpu.VMEM((ITERS, nsec, 3, 8, width), F32),
            pltpu.VMEM((8, width), F32),
            pltpu.VMEM((nseg, 8, width), F32),
            pltpu.VMEM((8, width), F32),
            dma((7,)),
            dma((CHUNKS,)),
            dma((CHUNKS, nz)),
            dma((CHUNKS, nz)),
            dma((CHUNKS, nz)),
            dma((CHUNKS, nsec)),
            dma((ITERS, nsec)),
            dma((ITERS, nsec)),
            dma((nseg,)),
            dma((nseg,)),
        ],
        compiler_params=pltpu.CompilerParams(
            collective_id=0, has_side_effects=True, vmem_limit_bytes=64 * 2**20
        ),
    )(x, env_build[0, 0], env_right[0, 0], left, right, charge, rank)
    return (state[None, None], energy.reshape(1), weight.reshape(1, 1))


def solution(mesh):
    return jax.shard_map(
        shards,
        mesh=mesh,
        in_specs=(
            P("seg", "sec", None, None, None),
            P("seg", "sec", None, None, None),
            P("seg", "sec", None, None, None),
            P(),
            P(),
            P(),
            P("sec"),
        ),
        out_specs=(P("seg", "sec", None, None, None), P("seg"), P("seg", "sec")),
        check_vma=False,
    )
```

time: 69.5 us -> 63.7 us (0.917)
  local copies, waits for them, and re-layouts: 6.62 us -> 1.89 us
  Pallas kernels: 57.6 us -> 56.8 us
    unnamed x13 -> x1, local copies, waits for them, and re-layouts: 6.42 us -> 1.89 us
    pallas_call x1, Pallas kernels: 57.6 us -> 56.8 us  [shards(): pl.pallas_call(functools.partial(kernel, nseg, nsec), out_shape=(jax.Shap...]
where the time goes in v2:
time: 63.7 us; the launch traced here: 63.4 us
  Pallas kernels  56.8 us (89%)
  between operations  4.75 us (7%)
  local copies, waits for them, and re-layouts  1.89 us (3%)
    pallas_call x1, Pallas kernels, shards(): pl.pallas_call(functools.partial(kernel, nseg, nsec), out_shape=(jax.Shap...  56.8 us
    unnamed x1, local copies, waits for them, and re-layouts  1.89 us

profile of v2, /device:TPU:4, one launch (start us, length us, event | category | flops | bytes accessed | tf_op | source)
XLA Modules:
  0.0 63.4 jit_solution(774392880985126523)
XLA Ops:
  1.3 56.8 %shard_map.94 = (bf16[16,128,128]{2,1,0:T(8,128)(2,1)}, f32[1,1]{1,0:T(1,128)}, f32[1,1]{1,0:T(1,128)}) custom-call(bf16[16,128,128]{2,1,0:T(8,128)(2,1)} %bitcast.7, bf16[12,128,128]{2,1,0:T(8,128)(2,1)} %bitcast.9, bf16[12,128,128]{2,1,0:T(8,128)(2,1)} %bitcast.10, bf16[12,4,4,12]{3,2,1,0:T(4,128)(2,1)} %bitcast.11, bf16[12,4,4,12]{3,2,1,0:T(4,128)(2,1)} %bitcast.12, ...), custom_call_target="tpu_custom_call" | custom-call | tf_op jit(solution)/shard_map/pallas_call | solution.py:414
  58.1 1.9 %copy.14 = bf16[1,1,16,128,128]{4,3,2,1,0:T(8,128)(2,1)} copy(bf16[1,1,16,128,128]{4,3,2,1,0:T(8,128)(2,1)} %bitcast.8) | data formatting | bytes 1048576

commit v3 on v2

--- a/solution.py
+++ b/solution.py
@@ -87,7 +87,7 @@
     nseg, nsec,
     psi_hbm, env_hbm, renv_hbm, left_hbm, right_hbm, charge_hbm, rank_hbm,
     state_ref, energy_ref, weight_ref,
-    l0, l1, l2, l3, own, psi_ref, env_ref, renv_ref, left_ref, right_ref, charge_ref, rank_ref, x1, x3a, x3b, mpo, stage, flat, xt, xq, acc,
+    l0, l1, l2, l3, own, psi_ref, env_ref, renv_ref, left_ref, right_ref, charge_ref, rank_ref, x1, x3a, x3b, mpo, stage, flat, xq, acc,
     sum_tx, sum_rx, share_tx, share_rx, run,
     load_sem, shift_sem, up_sem, down_sem, side_sem, recv_sem, sum_send, sum_recv, share_send, share_recv,
 ):
@@ -216,19 +216,14 @@
         for p in range(states):
             flat[pl.ds(p, rows, stride=states), :] = psi_ref[p, c * rows : (c + 1) * rows, :].astype(F32)
 
-    def right_apply():
-        xt[...] = flat[...].astype(BF16)
-
-        def one(w, carry):
+    def right_apply(at=0):
+        lhs = flat[at * rows * states : (at + 1) * rows * states, :].astype(BF16)
+        for w in range(renv_ref.shape[0] // 2):
             rhs = jnp.concatenate([renv_ref[2 * w], renv_ref[2 * w + 1]], axis=1)
-            out = dot(xt[...], rhs).astype(BF16)
+            out = dot(lhs, rhs).astype(BF16)
             for half in range(2):
-                x1[:, pl.ds(pl.multiple_of((2 * w + half) * states, states), states), :] = (
-                    out[:, half * width : (half + 1) * width].reshape(rows, states, width)
-                )
-            return carry
-
-        lax.fori_loop(0, renv_ref.shape[0] // 2, one, 0)
+                lo = (2 * w + half) * states
+                x1[:, lo : lo + states, :] = out[:, half * width : (half + 1) * width].reshape(rows, states, width)
 
     def mpo_apply(c, x3):
         group = 16
@@ -262,17 +257,20 @@
     def left_of(q):
         return lax.rem(sec - charge_ref[q] + nsec, nsec)
 
-    per = 4
+    per = 8
     zero = jnp.zeros((8, width), F32)
 
-    def first(c, squares, keep):
+    def first(half, squares, keep):
+        lo, some_rows = 2 * half * rows, 2 * rows
+
         def some(step, squares):
             for j in range(per):
                 q = step * per + j
-                h = dot(slots[c][left_of(q)], x3a[q])
-                u = jnp.where(keep, psi_ref[q, c * rows : (c + 1) * rows, :].astype(F32) - 0.5 * h, 0.0)
-                flat[pl.ds(q, rows, stride=states), :] = u
-                xq[q, c * rows : (c + 1) * rows, :] = u.astype(BF16)
+                s = left_of(q)
+                h = dot(jnp.concatenate([slots[2 * half][s], slots[2 * half + 1][s]], axis=0), x3a[q])
+                u = jnp.where(keep, psi_ref[q, lo : lo + some_rows, :].astype(F32) - 0.5 * h, 0.0)
+                flat[pl.ds(q, some_rows, stride=states), :] = u
+                xq[q, lo : lo + some_rows, :] = u.astype(BF16)
                 squares = squares + fold(u * u)
             return squares
 
@@ -306,27 +304,35 @@
     for load in loads[1:]:
         load.wait()
     mpo[...] = build_mpo(left_ref, right_ref, stage)
-    keep = iota((rows, width), 1) < rank_ref[0]
+    keep = iota((2 * rows, width), 1) < rank_ref[0]
     squares = zero
-    for t in range(CHUNKS + nz - 1):
-        for c in reversed(range(CHUNKS)):
-            if 0 <= t - c < nz:
-                hop(c, t - c)
-        if t < CHUNKS:
-            flatten(t)
-            right_apply()
-            mpo_apply(t, x3a)
-        c = t - nz + 1
-        if c >= 0:
-            settle(c)
-            squares = first(c, squares, keep)
-            if c == CHUNKS - 1:
-                sums = jnp.stack([squares, zero, zero])
-                sum_tx[0] = sums
-                sum_rx[0, sec] = sums
-                exchange(0)
-            right_apply()
-            mpo_apply(c, x3b)
+    finished = 2 * nz - 1
+    for t in range(finished + 1):
+        for c in range(CHUNKS):
+            if (t - c) % 2 == 0 and 0 <= (t - c) // 2 < nz:
+                hop(c, (t - c) // 2)
+        if t < 2 * CHUNKS:
+            if t % 2 == 0:
+                flatten(t // 2)
+                right_apply()
+            else:
+                mpo_apply(t // 2, x3a)
+    settle(0)
+    settle(1)
+    squares = first(0, squares, keep)
+    for c in range(2):
+        right_apply(c)
+        mpo_apply(c, x3b)
+        hop(c + 2, nz - 1)
+        settle(c + 2)
+    squares = first(1, squares, keep)
+    sums = jnp.stack([squares, zero, zero])
+    sum_tx[0] = sums
+    sum_rx[0, sec] = sums
+    exchange(0)
+    for c in range(2):
+        right_apply(c)
+        mpo_apply(c + 2, x3b)
 
     count = float(nsec * states * width * width)
     total = collect(0)
@@ -435,8 +441,7 @@
             pltpu.VMEM((states, bonds * width, width), BF16),
             pltpu.VMEM((bonds * states, bonds * states), BF16),
             pltpu.VMEM((bonds * states, 128), F32),
-            pltpu.VMEM((states * rows, width), F32),
-            pltpu.VMEM((states * rows, width), BF16),
+            pltpu.VMEM((2 * states * rows, width), F32),
             pltpu.VMEM((states, width, width), BF16),
             pltpu.VMEM((states, width, width), F32),
             pltpu.VMEM((ITERS, 3, 8, width), F32),

time: 63.7 us -> 61.8 us (0.970)
  Pallas kernels: 56.8 us -> 54.9 us
    pallas_call x1, Pallas kernels: 56.8 us -> 54.9 us  [shards(): pl.pallas_call(functools.partial(kernel, nseg, nsec), out_shape=(jax.Shap...]
where the time goes in v3:
time: 61.8 us; the launch traced here: 61.6 us
  Pallas kernels  54.9 us (89%)
  between operations  4.75 us (8%)
  local copies, waits for them, and re-layouts  1.89 us (3%)
    pallas_call x1, Pallas kernels, shards(): pl.pallas_call(functools.partial(kernel, nseg, nsec), out_shape=(jax.Shap...  54.9 us
    unnamed x1, local copies, waits for them, and re-layouts  1.89 us

profile of v3, /device:TPU:4, one launch (start us, length us, event | category | flops | bytes accessed | tf_op | source)
XLA Modules:
  0.0 61.6 jit_solution(8743539933099303683)
XLA Ops:
  1.3 54.9 %shard_map.94 = (bf16[16,128,128]{2,1,0:T(8,128)(2,1)}, f32[1,1]{1,0:T(1,128)}, f32[1,1]{1,0:T(1,128)}) custom-call(bf16[16,128,128]{2,1,0:T(8,128)(2,1)} %bitcast.7, bf16[12,128,128]{2,1,0:T(8,128)(2,1)} %bitcast.9, bf16[12,128,128]{2,1,0:T(8,128)(2,1)} %bitcast.10, bf16[12,4,4,12]{3,2,1,0:T(4,128)(2,1)} %bitcast.11, bf16[12,4,4,12]{3,2,1,0:T(4,128)(2,1)} %bitcast.12, ...), custom_call_target="tpu_custom_call" | custom-call | tf_op jit(solution)/shard_map/pallas_call | solution.py:420
  56.2 1.9 %copy.14 = bf16[1,1,16,128,128]{4,3,2,1,0:T(8,128)(2,1)} copy(bf16[1,1,16,128,128]{4,3,2,1,0:T(8,128)(2,1)} %bitcast.8) | data formatting | bytes 1048576

commit v4 on v3

--- a/solution.py
+++ b/solution.py
@@ -86,10 +86,10 @@
 def kernel(
     nseg, nsec,
     psi_hbm, env_hbm, renv_hbm, left_hbm, right_hbm, charge_hbm, rank_hbm,
-    state_ref, energy_ref, weight_ref,
-    l0, l1, l2, l3, own, psi_ref, env_ref, renv_ref, left_ref, right_ref, charge_ref, rank_ref, x1, x3a, x3b, mpo, stage, flat, xq, acc,
+    state_ref, scale_ref, energy_ref, weight_ref,
+    l0, l1, l2, l3, own, psi_ref, env_ref, renv_ref, left_ref, right_ref, charge_ref, rank_ref, x1, x3, mpo, stage, flat, xq, acc,
     sum_tx, sum_rx, share_tx, share_rx, run,
-    load_sem, shift_sem, up_sem, down_sem, side_sem, recv_sem, sum_send, sum_recv, share_send, share_recv,
+    load_sem, out_sem, shift_sem, up_sem, down_sem, side_sem, recv_sem, sum_send, sum_recv, share_send, share_recv,
 ):
     seg = lax.axis_index("seg")
     sec = lax.axis_index("sec")
@@ -213,11 +213,14 @@
                 side(c, 2 * h + core).wait_send()
 
     def flatten(c):
+        lo = pl.multiple_of(c * rows, rows)
+        at = lax.rem(c, 2) * rows * states
         for p in range(states):
-            flat[pl.ds(p, rows, stride=states), :] = psi_ref[p, c * rows : (c + 1) * rows, :].astype(F32)
-
-    def right_apply(at=0):
-        lhs = flat[at * rows * states : (at + 1) * rows * states, :].astype(BF16)
+            flat[pl.ds(at + p, rows, stride=states), :] = psi_ref[p, pl.ds(lo, rows), :].astype(F32)
+
+    def right_apply(c):
+        at = pl.multiple_of(lax.rem(c, 2) * rows * states, rows * states)
+        lhs = flat[pl.ds(at, rows * states), :].astype(BF16)
         for w in range(renv_ref.shape[0] // 2):
             rhs = jnp.concatenate([renv_ref[2 * w], renv_ref[2 * w + 1]], axis=1)
             out = dot(lhs, rhs).astype(BF16)
@@ -225,7 +228,7 @@
                 lo = (2 * w + half) * states
                 x1[:, lo : lo + states, :] = out[:, half * width : (half + 1) * width].reshape(rows, states, width)
 
-    def mpo_apply(c, x3):
+    def mpo_apply(c, turn):
         group = 16
         low = iota((states // 2, 8, width), 1) < 4
 
@@ -238,7 +241,7 @@
                 out = dot(operator, jnp.concatenate([x1[a + j], x1[a + j + 8]], axis=1))
                 parts = [out[:, :width], out[:, width:]]
                 heads = [part[:128].reshape(states, 8, width) for part in parts]
-                x3[:, pl.ds(pl.multiple_of(j * width + at, 16), 16), :] = jnp.concatenate(heads, axis=1).astype(BF16)
+                x3[turn, :, pl.ds(pl.multiple_of(j * width + at, 16), 16), :] = jnp.concatenate(heads, axis=1).astype(BF16)
                 return [part[128:].reshape(states // 2, 8, width) for part in parts]
 
             for j in range(4):
@@ -249,7 +252,7 @@
                 even = jnp.concatenate(evens, axis=1).astype(BF16)
                 odd = jnp.concatenate(odds, axis=1).astype(BF16)
                 both = jnp.stack([even, odd], axis=1).reshape(states, 16, width)
-                x3[:, pl.ds(pl.multiple_of((8 + j) * width + at, 16), 16), :] = both
+                x3[turn, :, pl.ds(pl.multiple_of((8 + j) * width + at, 16), 16), :] = both
             return carry
 
         lax.fori_loop(0, rows // group, one, 0)
@@ -260,21 +263,21 @@
     per = 8
     zero = jnp.zeros((8, width), F32)
 
-    def first(half, squares, keep):
+    def first(half, keep):
         lo, some_rows = 2 * half * rows, 2 * rows
 
         def some(step, squares):
             for j in range(per):
                 q = step * per + j
                 s = left_of(q)
-                h = dot(jnp.concatenate([slots[2 * half][s], slots[2 * half + 1][s]], axis=0), x3a[q])
+                h = dot(jnp.concatenate([slots[2 * half][s], slots[2 * half + 1][s]], axis=0), x3[0, q])
                 u = jnp.where(keep, psi_ref[q, lo : lo + some_rows, :].astype(F32) - 0.5 * h, 0.0)
                 flat[pl.ds(q, some_rows, stride=states), :] = u
                 xq[q, lo : lo + some_rows, :] = u.astype(BF16)
                 squares = squares + fold(u * u)
             return squares
 
-        return lax.fori_loop(0, states // per, some, squares)
+        sum_tx[0, 0] += lax.fori_loop(0, states // per, some, zero)
 
     def exchange(step):
         for d in range(1, nsec):
@@ -305,38 +308,64 @@
         load.wait()
     mpo[...] = build_mpo(left_ref, right_ref, stage)
     keep = iota((2 * rows, width), 1) < rank_ref[0]
-    squares = zero
     finished = 2 * nz - 1
-    for t in range(finished + 1):
+
+    def group(t):
         for c in range(CHUNKS):
             if (t - c) % 2 == 0 and 0 <= (t - c) // 2 < nz:
                 hop(c, (t - c) // 2)
-        if t < 2 * CHUNKS:
-            if t % 2 == 0:
-                flatten(t // 2)
-                right_apply()
-            else:
-                mpo_apply(t // 2, x3a)
-    settle(0)
-    settle(1)
-    squares = first(0, squares, keep)
-    for c in range(2):
+
+    def piece(i, carry):
+        c = lax.rem(i, CHUNKS)
+        for k in range(CHUNKS):
+            @pl.when(i == k)
+            def _():
+                group(2 * k)
+
+        @pl.when(i < CHUNKS)
+        def _():
+            flatten(c)
+
+        @pl.when(i == CHUNKS)
+        def _():
+            for t in range(2 * CHUNKS, finished + 1):
+                group(t)
+            settle(0)
+            settle(1)
+            first(0, keep)
+
+        @pl.when(i == CHUNKS + 1)
+        def _():
+            hop(2, nz - 1)
+
+        @pl.when(i == CHUNKS + 2)
+        def _():
+            hop(3, nz - 1)
+            settle(2)
+            settle(3)
+            first(1, keep)
+            sum_rx[0, sec] = sum_tx[0]
+            exchange(0)
+
         right_apply(c)
-        mpo_apply(c, x3b)
-        hop(c + 2, nz - 1)
-        settle(c + 2)
-    squares = first(1, squares, keep)
-    sums = jnp.stack([squares, zero, zero])
-    sum_tx[0] = sums
-    sum_rx[0, sec] = sums
-    exchange(0)
-    for c in range(2):
-        right_apply(c)
-        mpo_apply(c + 2, x3b)
+        for k in range(CHUNKS):
+            @pl.when(i == k)
+            def _():
+                group(2 * k + 1)
+
+        mpo_apply(c, i // CHUNKS)
+        return carry
+
+    sum_tx[0] = jnp.zeros_like(sum_tx[0])
+    lax.fori_loop(0, 2 * CHUNKS, piece, 0)
 
     count = float(nsec * states * width * width)
     total = collect(0)
     scale = lax.rsqrt(whole_sum(total[0]) / count + 1e-06)
+
+    def result(step):
+        some = pl.ds(step * per, per)
+        return pltpu.make_async_copy(acc.at[some], state_ref.at[some], out_sem.at[step])
 
     keep_all = iota((width, width), 1) < rank_ref[0]
 
@@ -345,13 +374,14 @@
         for j in range(per):
             q = step * per + j
             s = left_of(q)
-            h = dot(jnp.concatenate([slot[s] for slot in slots], axis=0), x3b[q]) * scale
+            h = dot(jnp.concatenate([slot[s] for slot in slots], axis=0), x3[1, q]) * scale
             x = xq[q].astype(F32) * scale
             u = jnp.where(keep_all, x - 0.5 * h, 0.0)
             acc[q] = u
             squares = squares + fold(u * u)
             inner = inner + fold(x * h)
             own_sum = own_sum + fold(x * x)
+        result(step).start()
         return squares, inner, own_sum
 
     sums = lax.fori_loop(0, states // per, last, (zero, zero, zero))
@@ -375,22 +405,8 @@
         def _():
             share_copy(d, False).start()
 
-    scale = lax.rsqrt(all_squares / count + 1e-06)
+    scale_ref[...] = lax.rsqrt(all_squares / count + 1e-06)
     energy_ref[...] = whole_sum(total[1]) / whole_sum(total[2])
-
-    def write(q, carry):
-        state_ref[q] = (acc[q] * scale).astype(BF16)
-        return carry
-
-    lax.fori_loop(0, states, write, 0)
-    run[...] = share_tx[...]
-    for d in range(1, nseg):
-        @pl.when(seg - d >= 0)
-        def _():
-            share_copy(d, True).wait_recv()
-            run[...] += share_rx[seg - d]
-
-    weight_ref[...] = run[0:1, 0:1]
     drain()
     for step in range(ITERS):
         for d in range(1, nsec):
@@ -402,6 +418,17 @@
         @pl.when(seg + d < nseg)
         def _():
             share_copy(d, False).wait_send()
+
+    run[...] = share_tx[...]
+    for d in range(1, nseg):
+        @pl.when(seg - d >= 0)
+        def _():
+            share_copy(d, True).wait_recv()
+            run[...] += share_rx[seg - d]
+
+    weight_ref[...] = run[0:1, 0:1]
+    for step in range(states // per):
+        result(step).wait()
 
 
 def shards(psi, env_build, env_right, site_left, site_right, charge, rank):
@@ -417,15 +444,16 @@
     nz = nsec // 2
     rows = width // CHUNKS
     slot = pltpu.VMEM((nsec, rows, bonds * width), BF16)
-    state, energy, weight = pl.pallas_call(
+    state, scale, energy, weight = pl.pallas_call(
         functools.partial(kernel, nseg, nsec),
         out_shape=(
-            jax.ShapeDtypeStruct(x.shape, BF16),
+            jax.ShapeDtypeStruct(x.shape, F32),
+            jax.ShapeDtypeStruct((1, 1), F32),
             jax.ShapeDtypeStruct((1, 1), F32),
             jax.ShapeDtypeStruct((1, 1), F32),
         ),
         in_specs=[hbm] * 7,
-        out_specs=(vmem, vmem, vmem),
+        out_specs=(hbm, vmem, vmem, vmem),
         scratch_shapes=[
             slot, slot, slot, slot,
             pltpu.VMEM((CHUNKS, rows, bonds * width), BF16),
@@ -437,8 +465,7 @@
             pltpu.SMEM(charge.shape, jnp.int32),
             pltpu.SMEM(rank.shape, jnp.int32),
             pltpu.VMEM((rows, bonds * states, width), BF16),
-            pltpu.VMEM((states, bonds * width, width), BF16),
-            pltpu.VMEM((states, bonds * width, width), BF16),
+            pltpu.VMEM((ITERS, states, bonds * width, width), BF16),
             pltpu.VMEM((bonds * states, bonds * states), BF16),
             pltpu.VMEM((bonds * states, 128), F32),
             pltpu.VMEM((2 * states * rows, width), F32),
@@ -450,6 +477,7 @@
             pltpu.VMEM((nseg, 8, width), F32),
             pltpu.VMEM((8, width), F32),
             dma((7,)),
+            dma((2,)),
             dma((CHUNKS,)),
             dma((CHUNKS, nz)),
             dma((CHUNKS, nz)),
@@ -464,6 +492,7 @@
             collective_id=0, has_side_effects=True, vmem_limit_bytes=64 * 2**20
         ),
     )(x, env_build[0, 0], env_right[0, 0], left, right, charge, rank)
+    state = (state * scale).astype(BF16)
     return (state[None, None], energy.reshape(1), weight.reshape(1, 1))
 
 

time: 61.8 us -> 61.4 us (level)
  other arithmetic: 0 us -> 2.7 us
  local copies, waits for them, and re-layouts: 1.89 us -> 0 us
  Pallas kernels: 54.9 us -> 53.7 us
    broadcast_in_dim x0 -> x1, other arithmetic: none -> 2.7 us  [shards(): return (state[None, None], energy.reshape(1), weight.reshape(1, 1))]
    unnamed x1 -> x0, local copies, waits for them, and re-layouts: 1.89 us -> none
    pallas_call x1, Pallas kernels: 54.9 us -> 53.7 us  [shards(): pl.pallas_call(functools.partial(kernel, nseg, nsec), out_shape=(jax.Shap...]
where the time goes in v4:
time: 61.4 us; the launch traced here: 61.2 us
  Pallas kernels  53.7 us (87%)
  between operations  4.81 us (8%)
  other arithmetic  2.7 us (4%)
    pallas_call x1, Pallas kernels, shards(): pl.pallas_call(functools.partial(kernel, nseg, nsec), out_shape=(jax.Shap...  53.7 us
    broadcast_in_dim x1, other arithmetic, shards(): return (state[None, None], energy.reshape(1), weight.reshape(1, 1))  2.7 us

profile of v4, /device:TPU:4, one launch (start us, length us, event | category | flops | bytes accessed | tf_op | source)
XLA Modules:
  0.0 61.2 jit_solution(17216307999678674265)
XLA Ops:
  1.3 53.7 %shard_map.94 = (f32[16,128,128]{2,1,0:T(8,128)}, f32[1,1]{1,0:T(1,128)}, f32[1,1]{1,0:T(1,128)}, f32[1,1]{1,0:T(1,128)}) custom-call(bf16[16,128,128]{2,1,0:T(8,128)(2,1)} %bitcast.9, bf16[12,128,128]{2,1,0:T(8,128)(2,1)} %bitcast.10, bf16[12,128,128]{2,1,0:T(8,128)(2,1)} %bitcast.11, bf16[12,4,4,12]{3,2,1,0:T(4,128)(2,1)} %bitcast.12, ...), custom_call_target="tpu_custom_call" | custom-call | tf_op jit(solution)/shard_map/pallas_call | solution.py:447
  55.0 2.7 %fusion = bf16[1,1,16,128,128]{4,3,2,1,0:T(8,128)(2,1)} fusion(f32[16,128,128]{2,1,0:T(8,128)} %get-tuple-element.7, f32[]{:T(128)} %bitcast.5), kind=kLoop, calls=%fused_computation.1 | loop fusion | flops 524288 | bytes 1572868 | tf_op jit(solution)/shard_map/broadcast_in_dim | solution.py:496

commit v5 on v4

--- a/solution.py
+++ b/solution.py
@@ -263,7 +263,7 @@
     per = 8
     zero = jnp.zeros((8, width), F32)
 
-    def first(half, keep):
+    def first(half, part, keep):
         lo, some_rows = 2 * half * rows, 2 * rows
 
         def some(step, squares):
@@ -277,7 +277,7 @@
                 squares = squares + fold(u * u)
             return squares
 
-        sum_tx[0, 0] += lax.fori_loop(0, states // per, some, zero)
+        sum_tx[0, 0] += some(part, zero)
 
     def exchange(step):
         for d in range(1, nsec):
@@ -308,19 +308,38 @@
         load.wait()
     mpo[...] = build_mpo(left_ref, right_ref, stage)
     keep = iota((2 * rows, width), 1) < rank_ref[0]
-    finished = 2 * nz - 1
-
-    def group(t):
-        for c in range(CHUNKS):
-            if (t - c) % 2 == 0 and 0 <= (t - c) // 2 < nz:
-                hop(c, (t - c) // 2)
+    end = nz - 1
+
+    def both(pair, h_lo, h_hi):
+        return [(c, h) for h in range(h_lo, h_hi) for c in pair]
+
+    before_right = {
+        0: [(0, 0)],
+        1: [(1, 1)],
+        2: [(0, 2)],
+        3: [(2, 0)],
+        4: [(3, 0), (1, end)],
+        5: [(2, 2)],
+        6: both((2, 3), 3, end) + [(2, end), (3, end)],
+    }
+    before_mpo = {
+        0: [(1, 0), (0, 1)],
+        2: both((0, 1), 2, end)[1:],
+        3: [(0, end)],
+        4: [(3, 1)],
+        5: [(3, 2)],
+    }
+
+    def hops(i, table):
+        for k, some in table.items():
+            @pl.when(i == k)
+            def _():
+                for c, h in some:
+                    hop(c, h)
 
     def piece(i, carry):
         c = lax.rem(i, CHUNKS)
-        for k in range(CHUNKS):
-            @pl.when(i == k)
-            def _():
-                group(2 * k)
+        hops(i, before_right)
 
         @pl.when(i < CHUNKS)
         def _():
@@ -328,31 +347,23 @@
 
         @pl.when(i == CHUNKS)
         def _():
-            for t in range(2 * CHUNKS, finished + 1):
-                group(t)
             settle(0)
             settle(1)
-            first(0, keep)
-
-        @pl.when(i == CHUNKS + 1)
-        def _():
-            hop(2, nz - 1)
+            first(0, 0, keep)
+            hop(2, 1)
+            first(0, 1, keep)
 
         @pl.when(i == CHUNKS + 2)
         def _():
-            hop(3, nz - 1)
             settle(2)
             settle(3)
-            first(1, keep)
+            first(1, 0, keep)
+            first(1, 1, keep)
             sum_rx[0, sec] = sum_tx[0]
             exchange(0)
 
         right_apply(c)
-        for k in range(CHUNKS):
-            @pl.when(i == k)
-            def _():
-                group(2 * k + 1)
-
+        hops(i, before_mpo)
         mpo_apply(c, i // CHUNKS)
         return carry
 
@@ -377,7 +388,7 @@
             h = dot(jnp.concatenate([slot[s] for slot in slots], axis=0), x3[1, q]) * scale
             x = xq[q].astype(F32) * scale
             u = jnp.where(keep_all, x - 0.5 * h, 0.0)
-            acc[q] = u
+            acc[q] = u.astype(BF16)
             squares = squares + fold(u * u)
             inner = inner + fold(x * h)
             own_sum = own_sum + fold(x * x)
@@ -447,7 +458,7 @@
     state, scale, energy, weight = pl.pallas_call(
         functools.partial(kernel, nseg, nsec),
         out_shape=(
-            jax.ShapeDtypeStruct(x.shape, F32),
+            jax.ShapeDtypeStruct(x.shape, BF16),
             jax.ShapeDtypeStruct((1, 1), F32),
             jax.ShapeDtypeStruct((1, 1), F32),
             jax.ShapeDtypeStruct((1, 1), F32),
@@ -470,7 +481,7 @@
             pltpu.VMEM((bonds * states, 128), F32),
             pltpu.VMEM((2 * states * rows, width), F32),
             pltpu.VMEM((states, width, width), BF16),
-            pltpu.VMEM((states, width, width), F32),
+            pltpu.VMEM((states, width, width), BF16),
             pltpu.VMEM((ITERS, 3, 8, width), F32),
             pltpu.VMEM((ITERS, nsec, 3, 8, width), F32),
             pltpu.VMEM((8, width), F32),
@@ -492,7 +503,7 @@
             collective_id=0, has_side_effects=True, vmem_limit_bytes=64 * 2**20
         ),
     )(x, env_build[0, 0], env_right[0, 0], left, right, charge, rank)
-    state = (state * scale).astype(BF16)
+    state = (state.astype(F32) * scale).astype(BF16)
     return (state[None, None], energy.reshape(1), weight.reshape(1, 1))
 
 

time: 61.4 us -> 59.7 us (0.972)
  Pallas kernels: 53.7 us -> 52.1 us
    pallas_call x1, Pallas kernels: 53.7 us -> 52.1 us  [shards(): pl.pallas_call(functools.partial(kernel, nseg, nsec), out_shape=(jax.Shap...]
where the time goes in v5:
time: 59.7 us; the launch traced here: 59.4 us
  Pallas kernels  52.1 us (87%)
  between operations  4.79 us (8%)
  other arithmetic  2.54 us (4%)
    pallas_call x1, Pallas kernels, shards(): pl.pallas_call(functools.partial(kernel, nseg, nsec), out_shape=(jax.Shap...  52.1 us
    broadcast_in_dim x1, other arithmetic, shards(): return (state[None, None], energy.reshape(1), weight.reshape(1, 1))  2.54 us

profile of v5, /device:TPU:4, one launch (start us, length us, event | category | flops | bytes accessed | tf_op | source)
XLA Modules:
  0.0 59.4 jit_solution(4987799581600760462)
XLA Ops:
  1.3 52.1 %shard_map.94 = (bf16[16,128,128]{2,1,0:T(8,128)(2,1)}, f32[1,1]{1,0:T(1,128)}, f32[1,1]{1,0:T(1,128)}, f32[1,1]{1,0:T(1,128)}) custom-call(bf16[16,128,128]{2,1,0:T(8,128)(2,1)} %bitcast.9, bf16[12,128,128]{2,1,0:T(8,128)(2,1)} %bitcast.10, bf16[12,128,128]{2,1,0:T(8,128)(2,1)} %bitcast.11, bf16[12,4,4,12]{3,2,1,0:T(4,128)(2,1)} %bitcast.12, ...), custom_call_target="tpu_custom_call" | custom-call | tf_op jit(solution)/shard_map/pallas_call | solution.py:458
  53.4 2.5 %fusion = bf16[1,1,16,128,128]{4,3,2,1,0:T(8,128)(2,1)} fusion(bf16[16,128,128]{2,1,0:T(8,128)(2,1)} %get-tuple-element.7, f32[]{:T(128)} %bitcast.5), kind=kLoop, calls=%fused_computation.1 | loop fusion | flops 786432 | bytes 1048580 | tf_op jit(solution)/shard_map/broadcast_in_dim | solution.py:507

commit v6 on v5

--- a/solution.py
+++ b/solution.py
@@ -306,7 +306,6 @@
         shift_out(c)
     for load in loads[1:]:
         load.wait()
-    mpo[...] = build_mpo(left_ref, right_ref, stage)
     keep = iota((2 * rows, width), 1) < rank_ref[0]
     end = nz - 1
 
@@ -364,6 +363,11 @@
 
         right_apply(c)
         hops(i, before_mpo)
+
+        @pl.when(i == 0)
+        def _():
+            mpo[...] = build_mpo(left_ref, right_ref, stage)
+
         mpo_apply(c, i // CHUNKS)
         return carry
 

time: 59.7 us -> 59.6 us (level)
  no operation moved by 1% of the time
where the time goes in v6:
time: 59.6 us; the launch traced here: 59.4 us
  Pallas kernels  52 us (87%)
  between operations  4.79 us (8%)
  other arithmetic  2.54 us (4%)
    pallas_call x1, Pallas kernels, shards(): pl.pallas_call(functools.partial(kernel, nseg, nsec), out_shape=(jax.Shap...  52 us
    broadcast_in_dim x1, other arithmetic, shards(): return (state[None, None], energy.reshape(1), weight.reshape(1, 1))  2.54 us

profile of v6, /device:TPU:4, one launch (start us, length us, event | category | flops | bytes accessed | tf_op | source)
XLA Modules:
  0.0 59.4 jit_solution(18100003034267396133)
XLA Ops:
  1.3 52.0 %shard_map.94 = (bf16[16,128,128]{2,1,0:T(8,128)(2,1)}, f32[1,1]{1,0:T(1,128)}, f32[1,1]{1,0:T(1,128)}, f32[1,1]{1,0:T(1,128)}) custom-call(bf16[16,128,128]{2,1,0:T(8,128)(2,1)} %bitcast.9, bf16[12,128,128]{2,1,0:T(8,128)(2,1)} %bitcast.10, bf16[12,128,128]{2,1,0:T(8,128)(2,1)} %bitcast.11, bf16[12,4,4,12]{3,2,1,0:T(4,128)(2,1)} %bitcast.12, ...), custom_call_target="tpu_custom_call" | custom-call | tf_op jit(solution)/shard_map/pallas_call | solution.py:462
  53.3 2.5 %fusion = bf16[1,1,16,128,128]{4,3,2,1,0:T(8,128)(2,1)} fusion(bf16[16,128,128]{2,1,0:T(8,128)(2,1)} %get-tuple-element.7, f32[]{:T(128)} %bitcast.5), kind=kLoop, calls=%fused_computation.1 | loop fusion | flops 786432 | bytes 1048580 | tf_op jit(solution)/shard_map/broadcast_in_dim | solution.py:511
